TPU v7x, 256 devices: a whole 4x4x8 slice. The times are simulated.
256 devices in a mesh: grp: 8 (over y, core), sub: 32 (over x, z).
Axes of the slice: x: 4, y: 4, z: 8, core: 2. Of those that a mesh axis runs over, the one named last changes fastest.
Arguments:
- right_side: float32 [65536, 2048], P(('grp', 'sub'))
- schur: bfloat16 [131072, 512], P(('grp', 'sub'))
- inv_factor: bfloat16 [131072, 512], P(('grp', 'sub'))
- coarse_inverse: float32 [2048, 256], P('grp')
- primal_index: int32 [256, 8], P(('grp', 'sub')), may hold values from 0 to 255
- phase: int32 [65536], P(('grp', 'sub')), may hold values from 0 to 3
- phase_coef: float32 [4], replicated, may hold values from 0.5 to 4
Outputs:
- solution: float32 [65536, 2048], P(('grp', 'sub'))
- residual: float32 [65536, 2048], P(('grp', 'sub'))
All inputs are finite; a program needn't handle non-finite values.
Results may differ from a plain program's by a relative error of at most 0.0056.
Values may be sent and summed in bfloat16 or wider, within the bound.
A program may use at most 64 MiB of HBM per device.

v0:
```python
import jax
import jax.numpy as jnp
from jax import lax
from jax.sharding import PartitionSpec as P


def shifted(value, axis, steps):
    count = lax.axis_size(axis)
    pairs = [(source, (source + steps) % count) for source in range(count)]
    return lax.ppermute(value, axis, pairs)


def transposed(matrix, operand):
    return lax.dot_general(
        matrix, operand, (((0,), (0,)), ((), ())), preferred_element_type=jnp.float32
    )


def body(right_side, schur, inv_factor, coarse_inverse, primal_index, phase, phase_coef):
    highest = lax.Precision.HIGHEST
    face_rows = right_side.shape[0]
    columns = jnp.arange(face_rows, dtype=jnp.int32)
    onehot = (primal_index[0][:, None] == columns[None, :]).astype(jnp.float32)
    primal_count = onehot.shape[0]
    resid_b = right_side.astype(jnp.bfloat16)
    left_resid = shifted(resid_b, "sub", 1)
    local_resid = jnp.concatenate([left_resid, resid_b], axis=0)
    first = jnp.dot(inv_factor, local_resid, preferred_element_type=jnp.float32).astype(
        jnp.bfloat16
    )
    second = transposed(inv_factor, first).astype(jnp.bfloat16)
    upper = second[:face_rows]
    from_right = shifted(upper, "sub", -1)
    lower = second[face_rows:]
    local_part = lower.astype(jnp.float32) + from_right.astype(jnp.float32)
    own_primal = jnp.dot(onehot, right_side, precision=highest)
    position = lax.axis_index("sub")
    group_primal = lax.all_gather(own_primal, "sub", axis=0, tiled=True)
    my_rows = lax.dynamic_slice_in_dim(coarse_inverse, position * primal_count, primal_count, 0)
    solved = jnp.dot(my_rows, group_primal, precision=highest)
    summed = lax.psum(solved, "grp")
    correction = solved + summed / lax.axis_size("grp")
    scattered = lax.dot_general(onehot, correction, (((0,), (0,)), ((), ())), precision=highest)
    direction = 0.5 * local_part + scattered
    dir_b = direction.astype(jnp.bfloat16)
    rz_part = jnp.sum(right_side * direction, axis=0)
    left_dir = shifted(dir_b, "sub", 1)
    image = jnp.dot(
        schur, jnp.concatenate([left_dir, dir_b], axis=0), preferred_element_type=jnp.float32
    ).astype(jnp.bfloat16)
    image_up = image[:face_rows]
    image_right = shifted(image_up, "sub", -1)
    image_low = image[face_rows:]
    phase_table = (
        phase[:, None] == jnp.arange(phase_coef.shape[0], dtype=jnp.int32)[None, :]
    ).astype(jnp.float32)
    coef_rows = jnp.dot(phase_table, phase_coef, precision=highest)
    dir_f = dir_b.astype(jnp.float32)
    qvec = (
        image_low.astype(jnp.float32) + image_right.astype(jnp.float32) + coef_rows[:, None] * dir_f
    )
    pq_part = jnp.sum(dir_f * qvec, axis=0)
    rz_total, pq_total = lax.psum((rz_part, pq_part), ("grp", "sub"))
    alpha = rz_total / pq_total
    return (alpha * dir_f, right_side - alpha * qvec)


def solution(mesh):
    in_specs = (
        P(("grp", "sub"), None),
        P(("grp", "sub"), None),
        P(("grp", "sub"), None),
        P("grp", None),
        P(("grp", "sub"), None),
        P(("grp", "sub")),
        P(),
    )
    out_specs = (P(("grp", "sub"), None), P(("grp", "sub"), None))
    return jax.shard_map(body, mesh=mesh, in_specs=in_specs, out_specs=out_specs, check_vma=False)
```

profile of v0, /device:TPU:1, one launch (start us, length us, event | category | flops | bytes accessed | tf_op | source)
XLA Modules:
  0.0 309.6 jit_solution(18175832615231809562)
XLA Ops:
  7.2 3.2 %fusion.21 = f32[8,2048]{1,0:T(8,128)} fusion(f32[256,2048]{1,0:T(8,128)} %param.7, s32[8]{0:T(128)} %bitcast.16), kind=kOutput, calls=%fused_computation.30 | convolution fusion | flops 50333696 | bytes 2162720 | tf_op jit(solution)/shard_map/dot_general | solution.py:36
  10.5 0.1 convert_element_type.39
  10.6 1.0 copy-done.6
  11.6 2.5 collective-permute-start
  14.1 30.4 %collective-permute-done = bf16[256,2048]{1,0:T(8,128)(2,1)} collective-permute-done((bf16[256,2048]{1,0:T(8,128)(2,1)S(1)}, bf16[256,2048]{1,0:T(8,128)(2,1)}, u32[]{:S(2)}, u32[]{:S(2)}) %collective-permute-start) | collective-permute-done | bytes 1048608 | tf_op jit(solution)/shard_map/ppermute | solution.py:10
  44.5 5.3 %fusion = bf16[512,2048]{1,0:T(8,128)(2,1)} fusion(bf16[512,512]{1,0:T(8,128)(2,1)S(1)} %copy-done, bf16[256,2048]{1,0:T(8,128)(2,1)} %copy-done.6, bf16[256,2048]{1,0:T(8,128)(2,1)} %collective-permute-done), kind=kOutput, calls=%fused_computation.6 | convolution fusion | flops 2153775104 | bytes 4718592 | tf_op jit(solution)/shard_map/dot_general | solution.py:14
  49.8 2.3 slice.17
  52.1 1.3 collective-permute-start.1
  53.4 40.2 %all-gather.2.cloned.1.call-done = f32[256,2048]{1,0:T(8,128)} async-done(((f32[8,2048]{1,0:T(8,128)}), f32[256,2048]{1,0:T(8,128)}) %all-gather.2.cloned.1.call-update) | async-done | bytes 2097168 | tf_op jit(solution)/shard_map/all_gather | solution.py:38
  93.6 3.3 %fusion.19 = f32[8,2048]{1,0:T(8,128)} fusion(f32[256,2048]{1,0:T(8,128)} %all-gather.2.cloned.1.call-done, f32[256,256]{1,0:T(8,128)} %param.10, s32[]{:T(128)S(6)} %select_n.3), kind=kOutput, calls=%fused_computation.27 | convolution fusion | flops 50331648 | bytes 2170884 | tf_op jit(solution)/shard_map/dot_general | solution.py:40
  96.9 63.8 %all-reduce.3.cloned.1.call-done = f32[8,2048]{1,0:T(8,128)} async-done(((f32[8,2048]{1,0:T(8,128)}), f32[8,2048]{1,0:T(8,128)}) %all-reduce.3.cloned.1.call-update) | async-done | bytes 65552 | tf_op jit(solution)/shard_map/psum | solution.py:41
  160.8 2.1 fusion.15
  162.9 1.9 multiply_reduce_fusion
  164.8 1.4 collective-permute-start.2
  166.2 24.6 %collective-permute-done.2 = bf16[256,2048]{1,0:T(8,128)(2,1)S(1)} collective-permute-done((bf16[256,2048]{1,0:T(8,128)(2,1)S(1)}, bf16[256,2048]{1,0:T(8,128)(2,1)S(1)}, u32[]{:S(2)}, u32[]{:S(2)}) %collective-permute-start.2) | collective-permute-done | bytes 1048608 | tf_op jit(solution)/shard_map/ppermute | solution.py:10
  190.8 1.3 fusion.1
  192.1 0.1 slice.19
  192.2 1.3 collective-permute-start.3
  193.5 0.2 fusion.13
  193.7 19.9 %collective-permute-done.3 = bf16[256,2048]{1,0:T(8,128)(2,1)S(1)} collective-permute-done((bf16[256,2048]{1,0:T(8,128)(2,1)S(1)}, bf16[256,2048]{1,0:T(8,128)(2,1)S(1)}, u32[]{:S(2)}, u32[]{:S(2)}) %collective-permute-start.3) | collective-permute-done | bytes 1048608 | tf_op jit(solution)/shard_map/ppermute | solution.py:10
  213.5 0.7 fusion.3
  214.2 0.3 copy-done.4
  214.5 83.4 %all-reduce = (f32[2048]{0:T(1024)S(1)}, f32[2048]{0:T(1024)S(1)}) all-reduce(f32[2048]{0:T(1024)S(1)} %get-tuple-element.4, f32[2048]{0:T(1024)S(1)} %fusion.3), channel_id=1, replica_groups=mesh['grp'=8,'sub'=32] {'grp','sub'}, use_global_device_ids=true, to_apply=%region_2.0 | all-reduce | flops 4096 | bytes 32768 | tf_op jit(solution)/shard_map/psum | solution.py:63
  298.0 4.8 %multiply_subtract_fusion = (f32[256,2048]{1,0:T(8,128)}, f32[256,2048]{1,0:T(8,128)}) fusion(f32[256,2048]{1,0:T(8,128)S(1)} %copy-done.1, bf16[256,2048]{1,0:T(8,128)(2,1)} %copy-done.2, bf16[256,2048]{1,0:T(8,128)(2,1)} %copy-done.4, f32[2048]{0:T(1024)S(1)} %div.11, f32[256]{0:T(256)S(1)} %bitcast.15, bf16[512,2048]{1,0:T(8,128)(2,1)} %copy-done.3), kind=kLoop, calls=%fused_computation.16 | loop fusion | flops 4718592 | bytes 9446400 | tf_op jit(solution)/shard_map/sub | solution.py:65
  (26 shorter events, 0.2 us)
Async XLA Ops:
  7.2 37.3 %copy-start = (bf16[512,512]{1,0:T(8,128)(2,1)S(1)}, bf16[512,512]{1,0:T(8,128)(2,1)}, u32[]{:S(2)}) copy-start(bf16[512,512]{1,0:T(8,128)(2,1)} %param.9) | copy-start | bytes 1572868
  7.2 3.3 %copy-start.1 = (f32[256,2048]{1,0:T(8,128)S(1)}, f32[256,2048]{1,0:T(8,128)}, u32[]{:S(2)}) copy-start(f32[256,2048]{1,0:T(8,128)} %param.7) | copy-start | bytes 6291460
  7.2 86.4 %all-gather.2.cloned.1.call-start = ((), (), s32[]{:S(2)}) async-start(), calls=%async_computation | async-start | bytes 2162688 | tf_op jit(solution)/shard_map/all_gather | solution.py:38
  10.4 150.3 %all-reduce.3.cloned.1.call-start = ((), (), s32[]{:S(2)}) async-start(), calls=%async_computation.1 | async-start | bytes 131072 | tf_op jit(solution)/shard_map/psum | solution.py:41
  10.6 1.0 copy-start.6
  11.6 32.9 %collective-permute-start = (bf16[256,2048]{1,0:T(8,128)(2,1)S(1)}, bf16[256,2048]{1,0:T(8,128)(2,1)}, u32[]{:S(2)}, u32[]{:S(2)}) collective-permute-start(bf16[256,2048]{1,0:T(8,128)(2,1)S(1)} %convert_element_type.39), channel_id=1, source_target_pairs={{0,1},{1,2},{2,3},{3,4},{4,5},{5,6},{6,7},{7,8},{8,9},{9,10},{10,1... | collective-permute-start | bytes 3145736 | tf_op jit(solution)/shard_map/ppermute | solution.py:10
  49.8 111.0 %copy-start.7 = (s32[1,8]{1,0:T(1,128)S(1)}, s32[1,8]{1,0:T(1,128)}, u32[]{:S(2)}) copy-start(s32[1,8]{1,0:T(1,128)} %param.11) | copy-start | bytes 100
  52.1 110.8 %collective-permute-start.1 = (bf16[256,2048]{1,0:T(8,128)(2,1)}, bf16[256,2048]{1,0:T(8,128)(2,1)}, u32[]{:S(2)}, u32[]{:S(2)}) collective-permute-start(bf16[256,2048]{1,0:T(8,128)(2,1)} %slice.17), channel_id=1, source_target_pairs={{0,31},{1,0},{2,1},{3,2},{4,3},{5,4},{6,5},{7,6},{8,7},{9,8},{10,9... | collective-permute-start | bytes 3145736 | tf_op jit(solution)/shard_map/ppermute | solution.py:10
  160.8 2.1 copy-start.5
  162.9 27.9 %copy-start.8 = (bf16[512,512]{1,0:T(8,128)(2,1)S(1)}, bf16[512,512]{1,0:T(8,128)(2,1)}, u32[]{:S(2)}) copy-start(bf16[512,512]{1,0:T(8,128)(2,1)} %param.8) | copy-start | bytes 1572868
  164.8 48.7 %copy-start.2 = (bf16[256,2048]{1,0:T(8,128)(2,1)}, bf16[256,2048]{1,0:T(8,128)(2,1)S(1)}, u32[]{:S(2)}) copy-start(bf16[256,2048]{1,0:T(8,128)(2,1)S(1)} %get-tuple-element.5) | copy-start | bytes 3145732
  164.8 25.9 %collective-permute-start.2 = (bf16[256,2048]{1,0:T(8,128)(2,1)S(1)}, bf16[256,2048]{1,0:T(8,128)(2,1)S(1)}, u32[]{:S(2)}, u32[]{:S(2)}) collective-permute-start(bf16[256,2048]{1,0:T(8,128)(2,1)S(1)} %get-tuple-element.5), channel_id=1, source_target_pairs={{0,1},{1,2},{2,3},{3,4},{4,5},{5,6},{6,7},{7,8},{8,9},{9,10},{10,1... | collective-permute-start | bytes 3145736 | tf_op jit(solution)/shard_map/ppermute | solution.py:10
  192.1 22.2 %copy-start.3 = (bf16[512,2048]{1,0:T(8,128)(2,1)}, bf16[512,2048]{1,0:T(8,128)(2,1)S(1)}, u32[]{:S(2)}) copy-start(bf16[512,2048]{1,0:T(8,128)(2,1)S(1)} %fusion.1) | copy-start | bytes 6291460
  192.1 1.4 copy-start.9
  192.1 1.4 copy-start.10
  192.2 21.3 %collective-permute-start.3 = (bf16[256,2048]{1,0:T(8,128)(2,1)S(1)}, bf16[256,2048]{1,0:T(8,128)(2,1)S(1)}, u32[]{:S(2)}, u32[]{:S(2)}) collective-permute-start(bf16[256,2048]{1,0:T(8,128)(2,1)S(1)} %slice.19), channel_id=1, source_target_pairs={{0,31},{1,0},{2,1},{3,2},{4,3},{5,4},{6,5},{7,6},{8,7},{9,8},{10,9... | collective-permute-start | bytes 3145736 | tf_op jit(solution)/shard_map/ppermute | solution.py:10
  213.5 1.0 copy-start.4
Sparse Core Ops, SparseCore 0:
  10.6 82.9 all-gather.1
  97.0 63.6 all-reduce.2
where the time goes:
time: 310 us
  waiting for transfers between devices  179 us (58%)
  blocking collectives  83.4 us (27%)
  matrix products  15.3 us (5%)
  between operations  14.2 us (5%)
  other arithmetic  7.52 us (2%)
  starting transfers between devices  6.44 us (2%)
  local copies, waits for them, and re-layouts  3.72 us (1%)
    psum x1, blocking collectives, body(): rz_total, pq_total = lax.psum((rz_part, pq_part), ('grp', 'sub'))  83.4 us
    ppermute x4, waiting for transfers between devices, shifted(): return lax.ppermute(value, axis, pairs)  74.9 us
    psum x1, waiting for transfers between devices, body(): summed = lax.psum(solved, 'grp')  63.8 us
    all_gather x1, waiting for transfers between devices, body(): group_primal = lax.all_gather(own_primal, 'sub', axis=0, tiled=True)  40.2 us
    ppermute x4, starting transfers between devices, shifted(): return lax.ppermute(value, axis, pairs)  6.36 us
  transfers between devices with their start and end apart: 6, of which 5 were waited for; matrix products, arithmetic and copies ran while one was open for 4% of the time, Pallas kernels for 0%

commit v1 on v0

v1 whole, which is shorter than its diff:
```python
import functools

import jax
import jax.numpy as jnp
from jax import lax
from jax.experimental import pallas as pl
from jax.experimental.pallas import tpu as pltpu
from jax.sharding import PartitionSpec as P

MESH = pl.DeviceIdType.MESH
F32 = jnp.float32
BF16 = jnp.bfloat16
CHUNK = 256
LANES = 128


def plan(mesh, width, chunk):
    groups, subs = mesh.shape["grp"], mesh.shape["sub"]
    depth = 8 if subs >= 16 else 2
    chunks = width // chunk
    return dict(
        groups=groups,
        subs=subs,
        zs=depth,
        xs=subs // depth,
        chunk=chunk,
        chunks=chunks,
        per=chunk // LANES,
        blocks=width // LANES,
        stride=max(1, subs // (width // LANES)),
        late=2,
    )


def kernel(cfg, rs_hbm, s_hbm, g_hbm, k_hbm, idx_ref, phase_ref, table_ref, sol_hbm, res_hbm, sc):
    groups, subs, zs, xs = cfg["groups"], cfg["subs"], cfg["zs"], cfg["xs"]
    chunk, chunks, per = cfg["chunk"], cfg["chunks"], cfg["per"]
    blocks, stride, late = cfg["blocks"], cfg["stride"], cfg["late"]
    early = chunks - late
    face = rs_hbm.shape[0]
    prim = idx_ref.shape[1]
    g = lax.axis_index("grp")
    j = lax.axis_index("sub")
    x, z = j // zs, lax.rem(j, zs)
    right = lax.rem(j + 1, subs)
    left = lax.rem(j + subs - 1, subs)
    low = pl.ds(face, face)
    up = pl.ds(0, face)

    def remote(src, dst, ssem, rsem, where):
        return pltpu.make_async_remote_copy(
            src_ref=src, dst_ref=dst, send_sem=ssem, recv_sem=rsem, device_id=where, device_id_type=MESH
        )

    def drain(ref, sem):
        pltpu.make_async_copy(ref, ref, sem).wait()

    def cols(c):
        return pl.ds(pl.multiple_of(c * chunk, chunk), chunk)

    def load_rs(c):
        return pltpu.make_async_copy(rs_hbm.at[:, cols(c)], sc["rs"].at[c], sc["rs_sem"].at[c])

    load_g = pltpu.make_async_copy(g_hbm, sc["gm"], sc["mat_sem"].at[0])
    load_k = pltpu.make_async_copy(k_hbm, sc["km"], sc["mat_sem"].at[1])
    load_s = pltpu.make_async_copy(s_hbm, sc["sm"], sc["mat_sem"].at[2])

    def rb_copy(c):
        return remote(
            sc["ext"].at[c, low], sc["ext"].at[c, up], sc["rb_ss"].at[c], sc["rb_rs"].at[c], {"sub": right}
        )

    def v_copy(c):
        return remote(sc["v"].at[c, up], sc["vr"].at[c], sc["v_ss"].at[c], sc["v_rs"].at[c], {"sub": left})

    def zb_copy(c):
        return remote(
            sc["dir"].at[c, low], sc["dir"].at[c, up], sc["zb_ss"].at[c], sc["zb_rs"].at[c], {"sub": right}
        )

    def y_copy(c):
        return remote(sc["y"].at[c, up], sc["yr"].at[c], sc["y_ss"].at[c], sc["y_rs"].at[c], {"sub": left})

    for c in range(chunks):
        load_rs(c).start()
    load_g.start()
    load_k.start()
    load_s.start()
    barrier = pltpu.get_barrier_semaphore()

    def greet_sub(d, carry):
        pl.semaphore_signal(barrier, inc=1, device_id={"sub": lax.rem(j + d, subs)}, device_id_type=MESH)
        return carry

    def greet_grp(d, carry):
        pl.semaphore_signal(barrier, inc=1, device_id={"grp": lax.rem(g + d, groups)}, device_id_type=MESH)
        return carry

    lax.fori_loop(1, subs, greet_sub, 0)
    lax.fori_loop(1, groups, greet_grp, 0)

    def cast(c):
        load_rs(c).wait()
        sc["ext"][c, low, :] = sc["rs"][c].astype(BF16)

    cast(0)
    pl.semaphore_wait(barrier, subs - 1 + groups - 1)
    rb_copy(0).start()

    def cast_rest(c, carry):
        cast(c)
        return carry

    def cast_send(c, carry):
        cast(c)
        rb_copy(c).start()
        return carry

    ahead = min(cfg.get("ahead", 3), chunks)
    lax.fori_loop(1, ahead, cast_send, 0)
    lax.fori_loop(ahead, chunks, cast_rest, 0)

    def pick(c, carry):
        for k in range(prim):
            row = sc["rs"][c, pl.ds(idx_ref[0, k], 1), :]
            for h in range(per):
                sc["rc"][c * per + h, k : k + 1, :] = row[:, h * LANES : (h + 1) * LANES]
        return carry

    lax.fori_loop(0, chunks, pick, 0)

    def rc_copy(b):
        return remote(
            sc["rc"].at[b], sc["rcin"].at[j], sc["rc_ss"].at[b], sc["rc_rs"], {"sub": b * stride}
        )

    def rc_send(b, carry):
        @pl.when(b * stride != j)
        def _():
            rc_copy(b).start()

        @pl.when(b * stride == j)
        def _():
            sc["rcin"][j] = sc["rc"][b]

        return carry

    lax.fori_loop(0, blocks, rc_send, 0)

    load_g.wait()
    sc["gt"][...] = sc["gm"][...].T
    lane = lax.broadcasted_iota(jnp.int32, (4 * prim, face), 1)
    sub_i = lax.broadcasted_iota(jnp.int32, (4 * prim, face), 0)
    which = jnp.full((4 * prim, face), -1, jnp.int32)
    for k in range(prim):
        which = jnp.where(lax.rem(sub_i, prim) == k, idx_ref[0, k], which)
    hot = jnp.where((lane == which) & (sub_i < 3 * prim), 1.0, 0.0).astype(F32)
    sc["pt"][...] = hot.T.astype(BF16)
    labels = phase_ref[...]
    coef = jnp.zeros(labels.shape, F32)
    for k in range(table_ref.shape[0]):
        coef = jnp.where(labels == k, table_ref[k], coef)
    sc["coef"][...] = jnp.broadcast_to(coef, (LANES, face)).T
    sc["ra"][...] = jnp.zeros_like(sc["ra"])

    def first(c, carry):
        rb_copy(c).wait_recv()

        @pl.when(c + ahead < chunks)
        def _():
            rb_copy(c + ahead).start()

        u = jnp.dot(sc["gm"][...], sc["ext"][c], preferred_element_type=F32).astype(BF16)
        sc["v"][c] = jnp.dot(sc["gt"][...], u, preferred_element_type=F32).astype(BF16)
        v_copy(c).start()
        return carry

    is_solver = (lax.rem(j, stride) == 0) & (j < blocks * stride)
    my_block = j // stride

    def h_copy(t):
        return remote(
            sc["hout"].at[t], sc["hin"].at[my_block], sc["h_ss"].at[t], sc["h_rs"], {"sub": t}
        )

    def solve():
        @pl.when(is_solver)
        def _():
            load_k.wait()
            drain(sc["rcin"].at[pl.ds(0, subs - 1)], sc["rc_rs"])
            rhs = sc["rcin"][...].reshape(subs * prim, LANES)
            h = jnp.dot(sc["km"][...], rhs, precision=lax.Precision.HIGHEST, preferred_element_type=F32)
            sc["hout"][...] = h.reshape(subs, prim, LANES)

            def h_send(d, carry):
                h_copy(lax.rem(j + d, subs)).start()
                return carry

            lax.fori_loop(1, subs, h_send, 0)
            sc["hin"][my_block] = sc["hout"][j]

        @pl.when(jnp.logical_not(is_solver))
        def _():
            load_k.wait()

    def g_copy(t):
        return remote(sc["hin"], sc["gin"].at[g], sc["g_ss"].at[t], sc["g_rs"], {"grp": t})

    def share():
        @pl.when(is_solver)
        def _():
            drain(sc["hin"].at[pl.ds(0, blocks - 1)], sc["h_rs"])

        @pl.when(jnp.logical_not(is_solver))
        def _():
            drain(sc["hin"], sc["h_rs"])

        def g_send(d, carry):
            g_copy(lax.rem(g + d, groups)).start()
            return carry

        lax.fori_loop(1, groups, g_send, 0)
        sc["gin"][g] = sc["hin"][...]

    def correct():
        drain(sc["gin"].at[pl.ds(0, groups - 1)], sc["g_rs"])
        for b in range(blocks):
            total = sc["gin"][0, b]
            for t in range(1, groups):
                total = total + sc["gin"][t, b]
            e = sc["hin"][b] + total / groups
            hi = e.astype(BF16).astype(F32)
            rest = e - hi
            mid = rest.astype(BF16).astype(F32)
            tail = rest - mid
            c, h = divmod(b, per)
            stack = jnp.concatenate([hi, mid, tail, jnp.zeros_like(hi)], axis=0)
            sc["e3"][c, :, h * LANES : (h + 1) * LANES] = stack.astype(BF16)

    def rows_to(ref, base, c, value):
        for h in range(per):
            ref[base + c * per + h] = value[:, h * LANES : (h + 1) * LANES]

    def direction(c, carry):
        v_copy(c).wait_recv()
        fix = jnp.dot(sc["pt"][...], sc["e3"][c], preferred_element_type=F32)
        both = sc["v"][c, low, :].astype(F32) + sc["vr"][c].astype(F32)
        zz = 0.5 * both + fix
        sc["dir"][c, low, :] = zz.astype(BF16)
        zb_copy(c).start()
        rows_to(sc["ra"], 0, c, jnp.sum(sc["rs"][c] * zz, axis=0, keepdims=True))
        return carry

    def wide_coef():
        return jnp.concatenate([sc["coef"][...]] * per, axis=1)

    def image(c, ref, base):
        zb_copy(c).wait_recv()
        y = jnp.dot(sc["sm"][...], sc["dir"][c], preferred_element_type=F32).astype(BF16)
        sc["y"][c] = y
        y_copy(c).start()
        zf = sc["dir"][c, low, :].astype(F32)
        part = jnp.sum(sc["dir"][c].astype(F32) * sc["y"][c].astype(F32), axis=0, keepdims=True)
        part = part + jnp.sum(wide_coef() * zf * zf, axis=0, keepdims=True)
        rows_to(ref, base, c, part)

    def finish(c, carry):
        y_copy(c).wait_recv()
        alpha = jnp.concatenate([sc["alpha"][c * per + h] for h in range(per)], axis=1)
        zf = sc["dir"][c, low, :].astype(F32)
        q = sc["y"][c, low, :].astype(F32) + sc["yr"][c].astype(F32) + wide_coef() * zf
        sc["sol"][c] = alpha * zf
        out_sol(c).start()
        sc["res"][c] = sc["rs"][c] - alpha * q
        out_res(c).start()
        return carry

    def out_sol(c):
        return pltpu.make_async_copy(sc["sol"].at[c], sol_hbm.at[:, cols(c)], sc["os"].at[c])

    def out_res(c):
        return pltpu.make_async_copy(sc["res"].at[c], res_hbm.at[:, cols(c)], sc["or"].at[c])

    span = sc["ra"].shape[0] // groups

    def exchange(name, count, me, where, src_of):
        def copy(t):
            return remote(src_of(t), sc[name].at[me], sc[name + "_ss"].at[t], sc[name + "_rs"], where(t))

        def start(own):
            def go(d, carry):
                copy(lax.rem(me + d, count)).start()
                return carry

            lax.fori_loop(1, count, go, 0)
            sc[name][me] = own

        def end():
            drain(sc[name].at[pl.ds(0, count - 1)], sc[name + "_rs"])
            total = sc[name][0]
            for t in range(1, count):
                total = total + sc[name][t]
            return total

        def sent():
            def go(d, carry):
                copy(lax.rem(me + d, count)).wait_send()
                return carry

            lax.fori_loop(1, count, go, 0)

        return start, end, sent

    to_grp = lambda t: {"grp": t}
    to_x = lambda t: {"sub": t * zs + z}
    to_z = lambda t: {"sub": x * zs + t}
    a1 = exchange("a1", groups, g, to_grp, lambda t: sc["ra"].at[pl.ds(t * span, span)])
    a2 = exchange("a2", xs, x, to_x, lambda t: sc["a2o"])
    a3 = exchange("a3", zs, z, to_z, lambda t: sc["a3o"])
    a4 = exchange("a4", groups, g, to_grp, lambda t: sc["a4o"])
    b1 = exchange("b1", groups, g, to_grp, lambda t: sc["rbt"])
    b2 = exchange("b2", xs, x, to_x, lambda t: sc["b2o"])
    b3 = exchange("b3", zs, z, to_z, lambda t: sc["b3o"])

    def hop(before, after, name):
        total = before[1]()
        sc[name][...] = total
        after[0](total)

    lax.fori_loop(0, chunks // 4, first, 0)
    solve()
    lax.fori_loop(chunks // 4, chunks // 2, first, 0)
    share()
    lax.fori_loop(chunks // 2, 3 * chunks // 4, first, 0)
    correct()
    lead = chunks - 3 * chunks // 4

    def first_dir(c, carry):
        direction(c - 3 * chunks // 4, 0)
        first(c, 0)
        return carry

    lax.fori_loop(3 * chunks // 4, chunks, first_dir, 0)
    load_s.wait()
    base = chunks * per

    def dir_image(c, carry):
        direction(c + lead, 0)
        image(c, sc["ra"], base)
        return carry

    lax.fori_loop(0, chunks - lead, dir_image, 0)
    for c in range(chunks - lead, early):
        image(c, sc["ra"], base)
    a1[0](sc["ra"][pl.ds(g * span, span)])
    for i in range(late):
        image(early + i, sc["rbt"], -early * per)
        if i == 0:
            hop(a1, a2, "a2o")
    b1[0](sc["rbt"][...])
    hop(a2, a3, "a3o")
    hop(b1, b2, "b2o")
    hop(a3, a4, "a4o")
    hop(b2, b3, "b3o")
    drain(sc["a4"].at[pl.ds(0, groups - 1)], sc["a4_rs"])
    for r in range(early * per):
        n, d = r, base + r
        sc["alpha"][r] = sc["a4"][n // span, n % span] / sc["a4"][d // span, d % span]
    lax.fori_loop(0, early, finish, 0)
    last = b3[1]()
    for r in range(late * per):
        n = early * per + r
        sc["alpha"][n] = sc["a4"][n // span, n % span] / last[r]
    lax.fori_loop(early, chunks, finish, 0)

    def drain_streams(c, carry):
        rb_copy(c).wait_send()
        v_copy(c).wait_send()
        zb_copy(c).wait_send()
        y_copy(c).wait_send()
        return carry

    lax.fori_loop(0, chunks, drain_streams, 0)

    def drain_rc(b, carry):
        @pl.when(b * stride != j)
        def _():
            rc_copy(b).wait_send()

        return carry

    lax.fori_loop(0, blocks, drain_rc, 0)

    @pl.when(is_solver)
    def _():
        def drain_h(d, carry):
            h_copy(lax.rem(j + d, subs)).wait_send()
            return carry

        lax.fori_loop(1, subs, drain_h, 0)

    def drain_g(d, carry):
        g_copy(lax.rem(g + d, groups)).wait_send()
        return carry

    lax.fori_loop(1, groups, drain_g, 0)
    for stage in (a1, a2, a3, a4, b1, b2, b3):
        stage[2]()

    def drain_out(c, carry):
        out_sol(c).wait()
        out_res(c).wait()
        return carry

    lax.fori_loop(0, chunks, drain_out, 0)


def scratch(cfg, face, prim):
    n, chunk, per = cfg["chunks"], cfg["chunk"], cfg["per"]
    groups, subs, xs, zs, blocks = cfg["groups"], cfg["subs"], cfg["xs"], cfg["zs"], cfg["blocks"]
    rows_a = (2 * n - cfg["late"]) * per
    span = -(-rows_a // groups)
    rows_b = cfg["late"] * per
    vm, dma = pltpu.VMEM, pltpu.SemaphoreType.DMA
    out = dict(
        rs=vm((n, face, chunk), F32),
        ext=vm((n, 2 * face, chunk), BF16),
        v=vm((n, 2 * face, chunk), BF16),
        vr=vm((n, face, chunk), BF16),
        dir=vm((n, 2 * face, chunk), BF16),
        y=vm((n, 2 * face, chunk), BF16),
        yr=vm((n, face, chunk), BF16),
        sol=vm((n, face, chunk), F32),
        res=vm((n, face, chunk), F32),
        gm=vm((2 * face, 2 * face), BF16),
        gt=vm((2 * face, 2 * face), BF16),
        sm=vm((2 * face, 2 * face), BF16),
        km=vm((subs * prim, subs * prim), F32),
        pt=vm((face, 4 * prim), BF16),
        coef=vm((face, LANES), F32),
        rc=vm((blocks, prim, LANES), F32),
        rcin=vm((subs, prim, LANES), F32),
        hout=vm((subs, prim, LANES), F32),
        hin=vm((blocks, prim, LANES), F32),
        gin=vm((groups, blocks, prim, LANES), F32),
        e3=vm((n, 4 * prim, chunk), BF16),
        alpha=vm((n * per, 1, LANES), F32),
        ra=vm((span * groups, 1, LANES), F32),
        rbt=vm((rows_b, 1, LANES), F32),
        a1=vm((groups, span, 1, LANES), F32),
        a2=vm((xs, span, 1, LANES), F32),
        a3=vm((zs, span, 1, LANES), F32),
        a4=vm((groups, span, 1, LANES), F32),
        a2o=vm((span, 1, LANES), F32),
        a3o=vm((span, 1, LANES), F32),
        a4o=vm((span, 1, LANES), F32),
        b1=vm((groups, rows_b, 1, LANES), F32),
        b2=vm((xs, rows_b, 1, LANES), F32),
        b3=vm((zs, rows_b, 1, LANES), F32),
        b2o=vm((rows_b, 1, LANES), F32),
        b3o=vm((rows_b, 1, LANES), F32),
        rs_sem=dma((n,)),
        mat_sem=dma((3,)),
        rc_ss=dma((blocks,)),
        rc_rs=dma(()),
        h_ss=dma((subs,)),
        h_rs=dma(()),
        g_ss=dma((groups,)),
        g_rs=dma(()),
        os=dma((n,)),
    )
    out["or"] = dma((n,))
    for name in ("rb", "v", "zb", "y"):
        out[name + "_ss"] = dma((n,))
        out[name + "_rs"] = dma((n,))
    for name, count in (("a1", groups), ("a2", xs), ("a3", zs), ("a4", groups), ("b1", groups), ("b2", xs), ("b3", zs)):
        out[name + "_ss"] = dma((count,))
        out[name + "_rs"] = dma(())
    return out


def solution(mesh, chunk=CHUNK):
    def body(right_side, schur, inv_factor, coarse_inverse, primal_index, phase, phase_coef):
        face, width = right_side.shape
        cfg = plan(mesh, width, chunk)
        shapes = scratch(cfg, face, primal_index.shape[1])
        keys = list(shapes)

        def wrapped(*refs):
            kernel(cfg, *refs[:9], dict(zip(keys, refs[9:])))

        anyspace = pl.BlockSpec(memory_space=pl.ANY)
        smem = pl.BlockSpec(memory_space=pltpu.SMEM)
        vmem = pl.BlockSpec(memory_space=pltpu.VMEM)
        out = jax.ShapeDtypeStruct((face, width), F32)
        return pl.pallas_call(
            wrapped,
            out_shape=(out, out),
            in_specs=[anyspace] * 4 + [smem, vmem, smem],
            out_specs=(anyspace, anyspace),
            scratch_shapes=[shapes[k] for k in keys],
            compiler_params=pltpu.CompilerParams(
                collective_id=0, has_side_effects=True, vmem_limit_bytes=44 * 1024 * 1024
            ),
            name="bddc_step",
        )(right_side, schur, inv_factor, coarse_inverse, primal_index, phase.reshape(1, face), phase_coef)

    both = ("grp", "sub")
    in_specs = (
        P(both, None),
        P(both, None),
        P(both, None),
        P("grp", None),
        P(both, None),
        P(both),
        P(),
    )
    out_specs = (P(both, None), P(both, None))
    return jax.shard_map(body, mesh=mesh, in_specs=in_specs, out_specs=out_specs, check_vma=False)
```

time: 310 us -> 90.5 us (0.29)
  waiting for transfers between devices: 179 us -> 0 us
  blocking collectives: 83.4 us -> 0 us
  Pallas kernels: 0 us -> 80.3 us
  matrix products: 15.3 us -> 0 us
  between operations: 14.2 us -> 0.66 us
  other arithmetic: 7.52 us -> 0 us
  starting transfers between devices: 6.44 us -> 0 us
  local copies, waits for them, and re-layouts: 3.72 us -> 9.24 us
    psum x1 -> x0, blocking collectives: 83.4 us -> none  [body(): rz_total, pq_total = lax.psum((rz_part, pq_part), ('grp', 'sub'))]
    pallas_call x0 -> x1, Pallas kernels: none -> 80.3 us  [body(): pl.pallas_call(wrapped, out_shape=(out, out), in_specs=[anyspace] * 4 + [...]
    ppermute x4 -> x0, waiting for transfers between devices: 74.9 us -> none  [shifted(): return lax.ppermute(value, axis, pairs)]
    psum x1 -> x0, waiting for transfers between devices: 63.8 us -> none  [body(): summed = lax.psum(solved, 'grp')]
    all_gather x1 -> x0, waiting for transfers between devices: 40.2 us -> none  [body(): group_primal = lax.all_gather(own_primal, 'sub', axis=0, tiled=True)]
    dot_general x6 -> x0, matrix products: 15.3 us -> none  [the longest x1 5.26 us: transposed(): lax.dot_general(matrix, operand, (((0,), (0,)), ((), ())), preferred_elem...]
    unnamed x22 -> x16, local copies, waits for them, and re-layouts: 1.3 us -> 9.24 us
    ppermute x4 -> x0, starting transfers between devices: 6.36 us -> none  [shifted(): return lax.ppermute(value, axis, pairs)]
  transfers between devices with their start and end apart: 6 -> 0, of which waited for: 5 -> 0; matrix products, arithmetic and copies ran while one was open for 4% -> 0% of each run, Pallas kernels for 0% -> 0%
where the time goes in v1:
time: 90.5 us; the launch traced here: 90.2 us
  Pallas kernels  80.3 us (89%)
  local copies, waits for them, and re-layouts  9.24 us (10%)
    pallas_call x1, Pallas kernels, body(): pl.pallas_call(wrapped, out_shape=(out, out), in_specs=[anyspace] * 4 + [...  80.3 us
    unnamed x16, local copies, waits for them, and re-layouts  9.24 us

profile of v1, /device:TPU:1, one launch (start us, length us, event | category | flops | bytes accessed | tf_op | source)
XLA Modules:
  0.0 90.2 jit_solution(15008645417456233752)
XLA Ops:
  0.6 0.0 copy-start
  0.6 1.6 %copy-done = f32[256,2048]{1,0:T(8,128)S(1)} copy-done((f32[256,2048]{1,0:T(8,128)S(1)}, f32[256,2048]{1,0:T(8,128)}, u32[]{:S(2)}) %copy-start) | copy-done | bytes 2097176
  2.2 0.0 copy-start.1
  2.2 1.0 %copy-done.1 = bf16[512,512]{1,0:T(8,128)(2,1)S(1)} copy-done((bf16[512,512]{1,0:T(8,128)(2,1)S(1)}, bf16[512,512]{1,0:T(8,128)(2,1)}, u32[]{:S(2)}) %copy-start.1) | copy-done | bytes 524312
  3.3 0.0 copy-start.2
  3.3 1.0 %copy-done.2 = bf16[512,512]{1,0:T(8,128)(2,1)S(1)} copy-done((bf16[512,512]{1,0:T(8,128)(2,1)S(1)}, bf16[512,512]{1,0:T(8,128)(2,1)}, u32[]{:S(2)}) %copy-start.2) | copy-done | bytes 524312
  4.3 0.0 copy-start.3
  4.3 0.9 %copy-done.3 = f32[256,256]{1,0:T(8,128)S(1)} copy-done((f32[256,256]{1,0:T(8,128)S(1)}, f32[256,256]{1,0:T(8,128)}, u32[]{:S(2)}) %copy-start.3) | copy-done | bytes 262168
  5.3 0.0 copy-start.4
  5.3 0.7 copy-done.4
  5.9 0.0 copy-start.5
  5.9 0.7 copy-done.5
  6.6 0.0 copy-start.6
  6.6 0.7 copy-done.6
  7.2 80.3 %bddc_step.1 = (f32[256,2048]{1,0:T(8,128)S(1)}, f32[256,2048]{1,0:T(8,128)S(1)}) custom-call(f32[256,2048]{1,0:T(8,128)S(1)} %copy-done, bf16[512,512]{1,0:T(8,128)(2,1)S(1)} %copy-done.1, bf16[512,512]{1,0:T(8,128)(2,1)S(1)} %copy-done.2, f32[256,256]{1,0:T(8,128)S(1)} %copy-done.3, s32[1,8]{1,0:T(1,128)S(1)} %copy-done.5, s32[1,256]{1,0:T(1,128)S(1)} %bitcast.1, ...), custom_call_target="tpu_custom_call" | custom-call | tf_op jit(solution)/shard_map/bddc_step/pallas_call | solution.py:496
  87.5 1.3 %copy.11 = f32[256,2048]{1,0:T(8,128)} copy(f32[256,2048]{1,0:T(8,128)S(1)} %get-tuple-element.4) | data formatting | bytes 4194304
  88.9 1.3 %copy.12 = f32[256,2048]{1,0:T(8,128)} copy(f32[256,2048]{1,0:T(8,128)S(1)} %get-tuple-element.5) | data formatting | bytes 4194304
Async XLA Ops:
  0.6 1.6 %copy-start = (f32[256,2048]{1,0:T(8,128)S(1)}, f32[256,2048]{1,0:T(8,128)}, u32[]{:S(2)}) copy-start(f32[256,2048]{1,0:T(8,128)} %refs_0_.1) | copy-start | bytes 6291460
  2.2 1.0 %copy-start.1 = (bf16[512,512]{1,0:T(8,128)(2,1)S(1)}, bf16[512,512]{1,0:T(8,128)(2,1)}, u32[]{:S(2)}) copy-start(bf16[512,512]{1,0:T(8,128)(2,1)} %refs_1_.1) | copy-start | bytes 1572868
  3.3 1.0 %copy-start.2 = (bf16[512,512]{1,0:T(8,128)(2,1)S(1)}, bf16[512,512]{1,0:T(8,128)(2,1)}, u32[]{:S(2)}) copy-start(bf16[512,512]{1,0:T(8,128)(2,1)} %refs_2_.1) | copy-start | bytes 1572868
  4.3 0.9 %copy-start.3 = (f32[256,256]{1,0:T(8,128)S(1)}, f32[256,256]{1,0:T(8,128)}, u32[]{:S(2)}) copy-start(f32[256,256]{1,0:T(8,128)} %refs_3_.1) | copy-start | bytes 786436
  5.3 0.7 copy-start.4
  5.9 0.7 copy-start.5
  6.6 0.7 copy-start.6

commit v2 on v1

--- a/solution.py
+++ b/solution.py
@@ -32,13 +32,14 @@
     )
 
 
-def kernel(cfg, rs_hbm, s_hbm, g_hbm, k_hbm, idx_ref, phase_ref, table_ref, sol_hbm, res_hbm, sc):
+def kernel(cfg, rs_hbm, s_hbm, g_hbm, k_hbm, idx_hbm, phase_hbm, table_hbm, sol_ref, res_ref, sc):
     groups, subs, zs, xs = cfg["groups"], cfg["subs"], cfg["zs"], cfg["xs"]
     chunk, chunks, per = cfg["chunk"], cfg["chunks"], cfg["per"]
     blocks, stride, late = cfg["blocks"], cfg["stride"], cfg["late"]
     early = chunks - late
     face = rs_hbm.shape[0]
-    prim = idx_ref.shape[1]
+    prim = idx_hbm.shape[1]
+    idx_ref, phase_ref, table_ref = sc["idx"], sc["phase"], sc["table"]
     g = lax.axis_index("grp")
     j = lax.axis_index("sub")
     x, z = j // zs, lax.rem(j, zs)
@@ -81,8 +82,16 @@
     def y_copy(c):
         return remote(sc["y"].at[c, up], sc["yr"].at[c], sc["y_ss"].at[c], sc["y_rs"].at[c], {"sub": left})
 
+    small = [
+        pltpu.make_async_copy(idx_hbm, idx_ref, sc["mat_sem"].at[3]),
+        pltpu.make_async_copy(phase_hbm, phase_ref, sc["mat_sem"].at[4]),
+        pltpu.make_async_copy(table_hbm, table_ref, sc["mat_sem"].at[5]),
+    ]
+
     for c in range(chunks):
         load_rs(c).start()
+    for load in small:
+        load.start()
     load_g.start()
     load_k.start()
     load_s.start()
@@ -116,7 +125,7 @@
         rb_copy(c).start()
         return carry
 
-    ahead = min(cfg.get("ahead", 3), chunks)
+    ahead = min(cfg.get("ahead", 2), chunks)
     lax.fori_loop(1, ahead, cast_send, 0)
     lax.fori_loop(ahead, chunks, cast_rest, 0)
 
@@ -127,6 +136,8 @@
                 sc["rc"][c * per + h, k : k + 1, :] = row[:, h * LANES : (h + 1) * LANES]
         return carry
 
+    for load in small:
+        load.wait()
     lax.fori_loop(0, chunks, pick, 0)
 
     def rc_copy(b):
@@ -158,8 +169,8 @@
     sc["pt"][...] = hot.T.astype(BF16)
     labels = phase_ref[...]
     coef = jnp.zeros(labels.shape, F32)
-    for k in range(table_ref.shape[0]):
-        coef = jnp.where(labels == k, table_ref[k], coef)
+    for k in range(table_ref.shape[1]):
+        coef = jnp.where(labels == k, table_ref[0, k], coef)
     sc["coef"][...] = jnp.broadcast_to(coef, (LANES, face)).T
     sc["ra"][...] = jnp.zeros_like(sc["ra"])
 
@@ -269,17 +280,9 @@
         alpha = jnp.concatenate([sc["alpha"][c * per + h] for h in range(per)], axis=1)
         zf = sc["dir"][c, low, :].astype(F32)
         q = sc["y"][c, low, :].astype(F32) + sc["yr"][c].astype(F32) + wide_coef() * zf
-        sc["sol"][c] = alpha * zf
-        out_sol(c).start()
-        sc["res"][c] = sc["rs"][c] - alpha * q
-        out_res(c).start()
-        return carry
-
-    def out_sol(c):
-        return pltpu.make_async_copy(sc["sol"].at[c], sol_hbm.at[:, cols(c)], sc["os"].at[c])
-
-    def out_res(c):
-        return pltpu.make_async_copy(sc["res"].at[c], res_hbm.at[:, cols(c)], sc["or"].at[c])
+        sol_ref[:, cols(c)] = alpha * zf
+        res_ref[:, cols(c)] = sc["rs"][c] - alpha * q
+        return carry
 
     span = sc["ra"].shape[0] // groups
 
@@ -319,8 +322,7 @@
     a3 = exchange("a3", zs, z, to_z, lambda t: sc["a3o"])
     a4 = exchange("a4", groups, g, to_grp, lambda t: sc["a4o"])
     b1 = exchange("b1", groups, g, to_grp, lambda t: sc["rbt"])
-    b2 = exchange("b2", xs, x, to_x, lambda t: sc["b2o"])
-    b3 = exchange("b3", zs, z, to_z, lambda t: sc["b3o"])
+    b2 = exchange("b2", subs, j, lambda t: {"sub": t}, lambda t: sc["b2o"])
 
     def hop(before, after, name):
         total = before[1]()
@@ -361,13 +363,12 @@
     hop(a2, a3, "a3o")
     hop(b1, b2, "b2o")
     hop(a3, a4, "a4o")
-    hop(b2, b3, "b3o")
     drain(sc["a4"].at[pl.ds(0, groups - 1)], sc["a4_rs"])
     for r in range(early * per):
         n, d = r, base + r
         sc["alpha"][r] = sc["a4"][n // span, n % span] / sc["a4"][d // span, d % span]
     lax.fori_loop(0, early, finish, 0)
-    last = b3[1]()
+    last = b2[1]()
     for r in range(late * per):
         n = early * per + r
         sc["alpha"][n] = sc["a4"][n // span, n % span] / last[r]
@@ -404,18 +405,11 @@
         return carry
 
     lax.fori_loop(1, groups, drain_g, 0)
-    for stage in (a1, a2, a3, a4, b1, b2, b3):
+    for stage in (a1, a2, a3, a4, b1, b2):
         stage[2]()
 
-    def drain_out(c, carry):
-        out_sol(c).wait()
-        out_res(c).wait()
-        return carry
-
-    lax.fori_loop(0, chunks, drain_out, 0)
-
-
-def scratch(cfg, face, prim):
+
+def scratch(cfg, face, prim, phases):
     n, chunk, per = cfg["chunks"], cfg["chunk"], cfg["per"]
     groups, subs, xs, zs, blocks = cfg["groups"], cfg["subs"], cfg["xs"], cfg["zs"], cfg["blocks"]
     rows_a = (2 * n - cfg["late"]) * per
@@ -430,8 +424,9 @@
         dir=vm((n, 2 * face, chunk), BF16),
         y=vm((n, 2 * face, chunk), BF16),
         yr=vm((n, face, chunk), BF16),
-        sol=vm((n, face, chunk), F32),
-        res=vm((n, face, chunk), F32),
+        idx=pltpu.SMEM((1, prim), jnp.int32),
+        phase=vm((1, face), jnp.int32),
+        table=pltpu.SMEM((1, phases), F32),
         gm=vm((2 * face, 2 * face), BF16),
         gt=vm((2 * face, 2 * face), BF16),
         sm=vm((2 * face, 2 * face), BF16),
@@ -455,25 +450,21 @@
         a3o=vm((span, 1, LANES), F32),
         a4o=vm((span, 1, LANES), F32),
         b1=vm((groups, rows_b, 1, LANES), F32),
-        b2=vm((xs, rows_b, 1, LANES), F32),
-        b3=vm((zs, rows_b, 1, LANES), F32),
+        b2=vm((subs, rows_b, 1, LANES), F32),
         b2o=vm((rows_b, 1, LANES), F32),
-        b3o=vm((rows_b, 1, LANES), F32),
         rs_sem=dma((n,)),
-        mat_sem=dma((3,)),
+        mat_sem=dma((6,)),
         rc_ss=dma((blocks,)),
         rc_rs=dma(()),
         h_ss=dma((subs,)),
         h_rs=dma(()),
         g_ss=dma((groups,)),
         g_rs=dma(()),
-        os=dma((n,)),
     )
-    out["or"] = dma((n,))
     for name in ("rb", "v", "zb", "y"):
         out[name + "_ss"] = dma((n,))
         out[name + "_rs"] = dma((n,))
-    for name, count in (("a1", groups), ("a2", xs), ("a3", zs), ("a4", groups), ("b1", groups), ("b2", xs), ("b3", zs)):
+    for name, count in (("a1", groups), ("a2", xs), ("a3", zs), ("a4", groups), ("b1", groups), ("b2", subs)):
         out[name + "_ss"] = dma((count,))
         out[name + "_rs"] = dma(())
     return out
@@ -483,27 +474,28 @@
     def body(right_side, schur, inv_factor, coarse_inverse, primal_index, phase, phase_coef):
         face, width = right_side.shape
         cfg = plan(mesh, width, chunk)
-        shapes = scratch(cfg, face, primal_index.shape[1])
+        shapes = scratch(cfg, face, primal_index.shape[1], phase_coef.shape[0])
         keys = list(shapes)
 
         def wrapped(*refs):
             kernel(cfg, *refs[:9], dict(zip(keys, refs[9:])))
 
-        anyspace = pl.BlockSpec(memory_space=pl.ANY)
-        smem = pl.BlockSpec(memory_space=pltpu.SMEM)
+        hbm = pl.BlockSpec(memory_space=pltpu.HBM)
         vmem = pl.BlockSpec(memory_space=pltpu.VMEM)
         out = jax.ShapeDtypeStruct((face, width), F32)
+        operands = (right_side, schur, inv_factor, coarse_inverse, primal_index)
+        operands += (phase.reshape(1, face), phase_coef.reshape(1, -1))
         return pl.pallas_call(
             wrapped,
             out_shape=(out, out),
-            in_specs=[anyspace] * 4 + [smem, vmem, smem],
-            out_specs=(anyspace, anyspace),
+            in_specs=[hbm] * 7,
+            out_specs=(vmem, vmem),
             scratch_shapes=[shapes[k] for k in keys],
             compiler_params=pltpu.CompilerParams(
                 collective_id=0, has_side_effects=True, vmem_limit_bytes=44 * 1024 * 1024
             ),
             name="bddc_step",
-        )(right_side, schur, inv_factor, coarse_inverse, primal_index, phase.reshape(1, face), phase_coef)
+        )(*[pltpu.with_memory_space_constraint(a, pltpu.HBM) for a in operands])
 
     both = ("grp", "sub")
     in_specs = (

time: 90.5 us -> 80.7 us (0.89)
  local copies, waits for them, and re-layouts: 9.24 us -> 2.64 us
  Pallas kernels: 80.3 us -> 77.3 us
    unnamed x16 -> x2, local copies, waits for them, and re-layouts: 9.24 us -> 2.64 us
    pallas_call x1, Pallas kernels: 80.3 us -> 77.3 us  [body(): pl.pallas_call(wrapped, out_shape=(out, out), in_specs=[hbm] * 7, out_spe...]
where the time goes in v2:
time: 80.7 us; the launch traced here: 80.6 us
  Pallas kernels  77.3 us (96%)
  local copies, waits for them, and re-layouts  2.64 us (3%)
    pallas_call x1, Pallas kernels, body(): pl.pallas_call(wrapped, out_shape=(out, out), in_specs=[hbm] * 7, out_spe...  77.3 us
    unnamed x2, local copies, waits for them, and re-layouts  2.64 us

profile of v2, /device:TPU:1, one launch (start us, length us, event | category | flops | bytes accessed | tf_op | source)
XLA Modules:
  0.0 80.6 jit_solution(16313963666880085136)
XLA Ops:
  0.6 77.3 %bddc_step.1 = (f32[256,2048]{1,0:T(8,128)S(1)}, f32[256,2048]{1,0:T(8,128)S(1)}) custom-call(f32[256,2048]{1,0:T(8,128)} %refs_0_.1, bf16[512,512]{1,0:T(8,128)(2,1)} %refs_1_.1, bf16[512,512]{1,0:T(8,128)(2,1)} %refs_2_.1, f32[256,256]{1,0:T(8,128)} %refs_3_.1, s32[1,8]{1,0:T(1,128)} %refs_4_.1, s32[1,256]{1,0:T(1,128)} %bitcast.2, f32[1,4]{1,0:T(1,128)} %bitcast.3), custom_call_target="tpu_custom_call" | custom-call | tf_op jit(solution)/shard_map/bddc_step/pallas_call | solution.py:488
  77.9 1.3 %copy.11 = f32[256,2048]{1,0:T(8,128)} copy(f32[256,2048]{1,0:T(8,128)S(1)} %get-tuple-element.4) | data formatting | bytes 4194304
  79.3 1.3 %copy.12 = f32[256,2048]{1,0:T(8,128)} copy(f32[256,2048]{1,0:T(8,128)S(1)} %get-tuple-element.5) | data formatting | bytes 4194304

commit v3 on v2

--- a/solution.py
+++ b/solution.py
@@ -12,11 +12,17 @@
 BF16 = jnp.bfloat16
 CHUNK = 256
 LANES = 128
+LATE = 3
+HOLD = 1
+HEAD = 0
+LEAD = 0
+AHEAD = 2
+ORDER = "wrmwrmSwHrmwrmWwrmwrmVwmCDDDwm"
 
 
 def plan(mesh, width, chunk):
     groups, subs = mesh.shape["grp"], mesh.shape["sub"]
-    depth = 8 if subs >= 16 else 2
+    depth = 8 if subs >= 16 else 4
     chunks = width // chunk
     return dict(
         groups=groups,
@@ -27,8 +33,11 @@
         chunks=chunks,
         per=chunk // LANES,
         blocks=width // LANES,
+        order=ORDER,
+        lead=LEAD,
         stride=max(1, subs // (width // LANES)),
-        late=2,
+        late=LATE,
+        head=HEAD,
     )
 
 
@@ -37,6 +46,7 @@
     chunk, chunks, per = cfg["chunk"], cfg["chunks"], cfg["per"]
     blocks, stride, late = cfg["blocks"], cfg["stride"], cfg["late"]
     early = chunks - late
+    head = cfg["head"]
     face = rs_hbm.shape[0]
     prim = idx_hbm.shape[1]
     idx_ref, phase_ref, table_ref = sc["idx"], sc["phase"], sc["table"]
@@ -97,12 +107,15 @@
     load_s.start()
     barrier = pltpu.get_barrier_semaphore()
 
+    def greet(sem, where):
+        pl.semaphore_signal(sem, inc=1, device_id=where, device_id_type=MESH)
+
+    def greet_grp(d, carry):
+        greet(barrier, {"grp": lax.rem(g + d, groups)})
+        return carry
+
     def greet_sub(d, carry):
-        pl.semaphore_signal(barrier, inc=1, device_id={"sub": lax.rem(j + d, subs)}, device_id_type=MESH)
-        return carry
-
-    def greet_grp(d, carry):
-        pl.semaphore_signal(barrier, inc=1, device_id={"grp": lax.rem(g + d, groups)}, device_id_type=MESH)
+        greet(barrier, {"sub": lax.rem(j + d, subs)})
         return carry
 
     lax.fori_loop(1, subs, greet_sub, 0)
@@ -112,22 +125,11 @@
         load_rs(c).wait()
         sc["ext"][c, low, :] = sc["rs"][c].astype(BF16)
 
-    cast(0)
-    pl.semaphore_wait(barrier, subs - 1 + groups - 1)
-    rb_copy(0).start()
-
-    def cast_rest(c, carry):
+    def cast_all(c, carry):
         cast(c)
         return carry
 
-    def cast_send(c, carry):
-        cast(c)
-        rb_copy(c).start()
-        return carry
-
-    ahead = min(cfg.get("ahead", 2), chunks)
-    lax.fori_loop(1, ahead, cast_send, 0)
-    lax.fori_loop(ahead, chunks, cast_rest, 0)
+    lax.fori_loop(0, chunks, cast_all, 0)
 
     def pick(c, carry):
         for k in range(prim):
@@ -156,7 +158,10 @@
 
         return carry
 
+    pl.semaphore_wait(barrier, groups - 1 + subs - 1)
     lax.fori_loop(0, blocks, rc_send, 0)
+    for c in range(AHEAD):
+        rb_copy(c).start()
 
     load_g.wait()
     sc["gt"][...] = sc["gm"][...].T
@@ -174,17 +179,14 @@
     sc["coef"][...] = jnp.broadcast_to(coef, (LANES, face)).T
     sc["ra"][...] = jnp.zeros_like(sc["ra"])
 
-    def first(c, carry):
-        rb_copy(c).wait_recv()
-
-        @pl.when(c + ahead < chunks)
-        def _():
-            rb_copy(c + ahead).start()
-
+    pt_copy = remote(sc["pt"], sc["ptl"], sc["el_ss"].at[0], sc["el_rs"].at[0], {"sub": right})
+    el_copy = remote(sc["el"], sc["ell"], sc["el_ss"].at[1], sc["el_rs"].at[1], {"sub": right})
+    if head:
+        pt_copy.start()
+    def first(c):
         u = jnp.dot(sc["gm"][...], sc["ext"][c], preferred_element_type=F32).astype(BF16)
         sc["v"][c] = jnp.dot(sc["gt"][...], u, preferred_element_type=F32).astype(BF16)
         v_copy(c).start()
-        return carry
 
     is_solver = (lax.rem(j, stride) == 0) & (j < blocks * stride)
     my_block = j // stride
@@ -203,6 +205,13 @@
             h = jnp.dot(sc["km"][...], rhs, precision=lax.Precision.HIGHEST, preferred_element_type=F32)
             sc["hout"][...] = h.reshape(subs, prim, LANES)
 
+        @pl.when(jnp.logical_not(is_solver))
+        def _():
+            load_k.wait()
+
+    def give():
+        @pl.when(is_solver)
+        def _():
             def h_send(d, carry):
                 h_copy(lax.rem(j + d, subs)).start()
                 return carry
@@ -210,12 +219,16 @@
             lax.fori_loop(1, subs, h_send, 0)
             sc["hin"][my_block] = sc["hout"][j]
 
-        @pl.when(jnp.logical_not(is_solver))
-        def _():
-            load_k.wait()
+    cores = 2
+    ys = groups // cores
+    row, core = g // cores, lax.rem(g, cores)
 
     def g_copy(t):
-        return remote(sc["hin"], sc["gin"].at[g], sc["g_ss"].at[t], sc["g_rs"], {"grp": t})
+        return remote(sc["hin"], sc["gin"].at[row], sc["g_ss"].at[t], sc["g_rs"], {"grp": t * cores + core})
+
+    pair_copy = remote(
+        sc["ysum"], sc["yother"], sc["p_ss"], sc["p_rs"], {"grp": row * cores + 1 - core}
+    )
 
     def share():
         @pl.when(is_solver)
@@ -226,50 +239,71 @@
         def _():
             drain(sc["hin"], sc["h_rs"])
 
-        def g_send(d, carry):
-            g_copy(lax.rem(g + d, groups)).start()
-            return carry
-
-        lax.fori_loop(1, groups, g_send, 0)
-        sc["gin"][g] = sc["hin"][...]
+        for d in range(1, ys):
+            g_copy(lax.rem(row + d, ys)).start()
+        sc["gin"][row] = sc["hin"][...]
+
+    def pair():
+        if ys > 1:
+            drain(sc["gin"].at[pl.ds(0, ys - 1)], sc["g_rs"])
+        total = sc["gin"][0]
+        for t in range(1, ys):
+            total = total + sc["gin"][t]
+        sc["ysum"][...] = total
+        pair_copy.start()
+
+    def split(e):
+        hi = e.astype(BF16).astype(F32)
+        rest = e - hi
+        mid = rest.astype(BF16).astype(F32)
+        tail = rest - mid
+        return jnp.concatenate([hi, mid, tail, jnp.zeros_like(hi)], axis=0).astype(BF16)
 
     def correct():
-        drain(sc["gin"].at[pl.ds(0, groups - 1)], sc["g_rs"])
+        pair_copy.wait_recv()
         for b in range(blocks):
-            total = sc["gin"][0, b]
-            for t in range(1, groups):
-                total = total + sc["gin"][t, b]
+            total = sc["ysum"][b] + sc["yother"][b]
             e = sc["hin"][b] + total / groups
-            hi = e.astype(BF16).astype(F32)
-            rest = e - hi
-            mid = rest.astype(BF16).astype(F32)
-            tail = rest - mid
             c, h = divmod(b, per)
-            stack = jnp.concatenate([hi, mid, tail, jnp.zeros_like(hi)], axis=0)
-            sc["e3"][c, :, h * LANES : (h + 1) * LANES] = stack.astype(BF16)
+            sc["e3"][c, :, h * LANES : (h + 1) * LANES] = split(e)
+            if c < head:
+                sc["el"][b] = e
+        if head:
+            el_copy.start()
 
     def rows_to(ref, base, c, value):
         for h in range(per):
             ref[base + c * per + h] = value[:, h * LANES : (h + 1) * LANES]
 
-    def direction(c, carry):
+    def low_copy(c):
+        return remote(
+            sc["v"].at[c, low], sc["dir"].at[c, up], sc["zb_ss"].at[c], sc["zb_rs"].at[c], {"sub": right}
+        )
+
+    def left_direction(c):
+        stack = [split(sc["ell"][c * per + h]) for h in range(per)]
+        fix = jnp.dot(sc["ptl"][...], jnp.concatenate(stack, axis=1), preferred_element_type=F32)
+        both = sc["dir"][c, up, :].astype(F32) + sc["v"][c, up, :].astype(F32)
+        sc["dir"][c, up, :] = (0.5 * both + fix).astype(BF16)
+
+    def direction(c, send=True):
         v_copy(c).wait_recv()
         fix = jnp.dot(sc["pt"][...], sc["e3"][c], preferred_element_type=F32)
         both = sc["v"][c, low, :].astype(F32) + sc["vr"][c].astype(F32)
         zz = 0.5 * both + fix
         sc["dir"][c, low, :] = zz.astype(BF16)
-        zb_copy(c).start()
+        if send:
+            zb_copy(c).start()
         rows_to(sc["ra"], 0, c, jnp.sum(sc["rs"][c] * zz, axis=0, keepdims=True))
-        return carry
 
     def wide_coef():
         return jnp.concatenate([sc["coef"][...]] * per, axis=1)
 
-    def image(c, ref, base):
-        zb_copy(c).wait_recv()
+    def image(c, ref, base, send=True):
         y = jnp.dot(sc["sm"][...], sc["dir"][c], preferred_element_type=F32).astype(BF16)
         sc["y"][c] = y
-        y_copy(c).start()
+        if send:
+            y_copy(c).start()
         zf = sc["dir"][c, low, :].astype(F32)
         part = jnp.sum(sc["dir"][c].astype(F32) * sc["y"][c].astype(F32), axis=0, keepdims=True)
         part = part + jnp.sum(wide_coef() * zf * zf, axis=0, keepdims=True)
@@ -329,39 +363,60 @@
         sc[name][...] = total
         after[0](total)
 
-    lax.fori_loop(0, chunks // 4, first, 0)
-    solve()
-    lax.fori_loop(chunks // 4, chunks // 2, first, 0)
-    share()
-    lax.fori_loop(chunks // 2, 3 * chunks // 4, first, 0)
-    correct()
-    lead = chunks - 3 * chunks // 4
-
-    def first_dir(c, carry):
-        direction(c - 3 * chunks // 4, 0)
-        first(c, 0)
-        return carry
-
-    lax.fori_loop(3 * chunks // 4, chunks, first_dir, 0)
+    count = {"w": 0, "m": 0, "r": AHEAD, "L": 0, "D": 0}
+    actions = {
+        "w": lambda c: rb_copy(c).wait_recv(),
+        "m": first,
+        "r": lambda c: rb_copy(c).start(),
+        "L": lambda c: low_copy(c).start(),
+        "D": lambda c: direction(c, send=c >= head),
+    }
+    steps = {"S": solve, "H": give, "W": share, "V": pair, "C": correct}
+    lead = cfg["lead"]
+    for step in cfg["order"]:
+        if step in steps:
+            steps[step]()
+        else:
+            actions[step](count[step])
+            count[step] += 1
     load_s.wait()
     base = chunks * per
 
-    def dir_image(c, carry):
-        direction(c + lead, 0)
-        image(c, sc["ra"], base)
-        return carry
-
-    lax.fori_loop(0, chunks - lead, dir_image, 0)
-    for c in range(chunks - lead, early):
-        image(c, sc["ra"], base)
-    a1[0](sc["ra"][pl.ds(g * span, span)])
-    for i in range(late):
-        image(early + i, sc["rbt"], -early * per)
-        if i == 0:
+    ready = max(head, count["D"])
+    for c in range(ready, min(chunks, ready + lead)):
+        direction(c)
+    ready = min(chunks, ready + lead)
+    if head:
+        pt_copy.wait_recv()
+        el_copy.wait_recv()
+    for c in range(chunks):
+        if c == early:
+            a1[0](sc["ra"][pl.ds(g * span, span)])
+        if c == early + 1:
             hop(a1, a2, "a2o")
+        if c == early + 2:
+            hop(a2, a3, "a3o")
+        if c < head and c >= count["D"]:
+            direction(c, send=False)
+        if ready < chunks and c >= head:
+            direction(ready)
+            ready += 1
+        zb_copy(c).wait_recv()
+        if c < head:
+            left_direction(c)
+        if ready < chunks and c < head:
+            direction(ready)
+            ready += 1
+        if c < early:
+            image(c, sc["ra"], base)
+        else:
+            image(c, sc["rbt"], -early * per, send=c < chunks - HOLD)
     b1[0](sc["rbt"][...])
-    hop(a2, a3, "a3o")
+    if late < 3:
+        hop(a2, a3, "a3o")
     hop(b1, b2, "b2o")
+    for c in range(chunks - HOLD, chunks):
+        y_copy(c).start()
     hop(a3, a4, "a4o")
     drain(sc["a4"].at[pl.ds(0, groups - 1)], sc["a4_rs"])
     for r in range(early * per):
@@ -374,6 +429,10 @@
         sc["alpha"][n] = sc["a4"][n // span, n % span] / last[r]
     lax.fori_loop(early, chunks, finish, 0)
 
+    if head:
+        pt_copy.wait_send()
+        el_copy.wait_send()
+
     def drain_streams(c, carry):
         rb_copy(c).wait_send()
         v_copy(c).wait_send()
@@ -400,13 +459,22 @@
 
         lax.fori_loop(1, subs, drain_h, 0)
 
-    def drain_g(d, carry):
-        g_copy(lax.rem(g + d, groups)).wait_send()
-        return carry
-
-    lax.fori_loop(1, groups, drain_g, 0)
+    for d in range(1, ys):
+        g_copy(lax.rem(row + d, ys)).wait_send()
+    pair_copy.wait_send()
     for stage in (a1, a2, a3, a4, b1, b2):
         stage[2]()
+
+
+def write_out(sol_ref, res_ref, sol_hbm, res_hbm, sems):
+    copies = [
+        pltpu.make_async_copy(sol_ref, sol_hbm, sems.at[0]),
+        pltpu.make_async_copy(res_ref, res_hbm, sems.at[1]),
+    ]
+    for copy in copies:
+        copy.start()
+    for copy in copies:
+        copy.wait()
 
 
 def scratch(cfg, face, prim, phases):
@@ -424,6 +492,11 @@
         dir=vm((n, 2 * face, chunk), BF16),
         y=vm((n, 2 * face, chunk), BF16),
         yr=vm((n, face, chunk), BF16),
+        ptl=vm((face, 4 * prim), BF16),
+        el=vm((max(cfg["head"], 1) * per, prim, LANES), F32),
+        ell=vm((max(cfg["head"], 1) * per, prim, LANES), F32),
+        el_ss=dma((2,)),
+        el_rs=dma((2,)),
         idx=pltpu.SMEM((1, prim), jnp.int32),
         phase=vm((1, face), jnp.int32),
         table=pltpu.SMEM((1, phases), F32),
@@ -437,7 +510,9 @@
         rcin=vm((subs, prim, LANES), F32),
         hout=vm((subs, prim, LANES), F32),
         hin=vm((blocks, prim, LANES), F32),
-        gin=vm((groups, blocks, prim, LANES), F32),
+        gin=vm((groups // 2, blocks, prim, LANES), F32),
+        ysum=vm((blocks, prim, LANES), F32),
+        yother=vm((blocks, prim, LANES), F32),
         e3=vm((n, 4 * prim, chunk), BF16),
         alpha=vm((n * per, 1, LANES), F32),
         ra=vm((span * groups, 1, LANES), F32),
@@ -458,7 +533,9 @@
         rc_rs=dma(()),
         h_ss=dma((subs,)),
         h_rs=dma(()),
-        g_ss=dma((groups,)),
+        g_ss=dma((groups // 2,)),
+        p_ss=dma(()),
+        p_rs=dma(()),
         g_rs=dma(()),
     )
     for name in ("rb", "v", "zb", "y"):
@@ -485,9 +562,10 @@
         out = jax.ShapeDtypeStruct((face, width), F32)
         operands = (right_side, schur, inv_factor, coarse_inverse, primal_index)
         operands += (phase.reshape(1, face), phase_coef.reshape(1, -1))
-        return pl.pallas_call(
+        held = pltpu.VMEM((face, width), F32)
+        results = pl.pallas_call(
             wrapped,
-            out_shape=(out, out),
+            out_shape=(held, held),
             in_specs=[hbm] * 7,
             out_specs=(vmem, vmem),
             scratch_shapes=[shapes[k] for k in keys],
@@ -496,6 +574,15 @@
             ),
             name="bddc_step",
         )(*[pltpu.with_memory_space_constraint(a, pltpu.HBM) for a in operands])
+        return pl.pallas_call(
+            write_out,
+            out_shape=(out, out),
+            in_specs=[vmem, vmem],
+            out_specs=(hbm, hbm),
+            scratch_shapes=[pltpu.SemaphoreType.DMA((2,))],
+            compiler_params=pltpu.CompilerParams(vmem_limit_bytes=1024 * 1024),
+            name="write_out",
+        )(*results)
 
     both = ("grp", "sub")
     in_specs = (

time: 80.7 us -> 78.6 us (0.974)
  local copies, waits for them, and re-layouts: 2.64 us -> 0 us
    unnamed x2 -> x0, local copies, waits for them, and re-layouts: 2.64 us -> none
    pallas_call x1 -> x2, Pallas kernels: 77.3 us -> 77.9 us  [the longest x1 75.8 us: body(): pl.pallas_call(wrapped, out_shape=(held, held), in_specs=[hbm] * 7, out_s...]
where the time goes in v3:
time: 78.6 us; the launch traced here: 78.5 us
  Pallas kernels  77.9 us (99%)
    pallas_call x1, Pallas kernels, body(): pl.pallas_call(wrapped, out_shape=(held, held), in_specs=[hbm] * 7, out_s...  75.8 us
    pallas_call x1, Pallas kernels, body(): pl.pallas_call(write_out, out_shape=(out, out), in_specs=[vmem, vmem], ou...  2.03 us

profile of v3, /device:TPU:1, one launch (start us, length us, event | category | flops | bytes accessed | tf_op | source)
XLA Modules:
  0.0 78.5 jit_solution(15655104317556669349)
XLA Ops:
  0.6 75.8 %bddc_step.1 = (f32[256,2048]{1,0:T(8,128)S(1)}, f32[256,2048]{1,0:T(8,128)S(1)}) custom-call(f32[256,2048]{1,0:T(8,128)} %refs_0_.1, bf16[512,512]{1,0:T(8,128)(2,1)} %refs_1_.1, bf16[512,512]{1,0:T(8,128)(2,1)} %refs_2_.1, f32[256,256]{1,0:T(8,128)} %refs_3_.1, s32[1,8]{1,0:T(1,128)} %refs_4_.1, s32[1,256]{1,0:T(1,128)} %bitcast.2, f32[1,4]{1,0:T(1,128)} %bitcast.3), custom_call_target="tpu_custom_call" | custom-call | tf_op jit(solution)/shard_map/bddc_step/pallas_call | solution.py:566
  76.5 2.0 %write_out.1 = (f32[256,2048]{1,0:T(8,128)}, f32[256,2048]{1,0:T(8,128)}) custom-call(f32[256,2048]{1,0:T(8,128)S(1)} %get-tuple-element.4.sol_ref, f32[256,2048]{1,0:T(8,128)S(1)} %get-tuple-element.5.res_ref), custom_call_target="tpu_custom_call" | custom-call | tf_op jit(solution)/shard_map/write_out/pallas_call | solution.py:577

commit v4 on v3

--- a/solution.py
+++ b/solution.py
@@ -13,11 +13,11 @@
 CHUNK = 256
 LANES = 128
 LATE = 3
-HOLD = 1
+HOLD = 0
 HEAD = 0
 LEAD = 0
 AHEAD = 2
-ORDER = "wrmwrmSwHrmwrmWwrmwrmVwmCDDDwm"
+ORDER = "wrmwSHrmwrmwrmWwrmVwrmCDDwmDwm"
 
 
 def plan(mesh, width, chunk):
@@ -98,6 +98,21 @@
         pltpu.make_async_copy(table_hbm, table_ref, sc["mat_sem"].at[5]),
     ]
 
+    barrier = pltpu.get_barrier_semaphore()
+
+    def greet(sem, where):
+        pl.semaphore_signal(sem, inc=1, device_id=where, device_id_type=MESH)
+
+    def greet_grp(d, carry):
+        greet(barrier, {"grp": lax.rem(g + d, groups)})
+        return carry
+
+    def greet_sub(d, carry):
+        greet(barrier, {"sub": lax.rem(j + 1 + lax.rem(d + subs // 3, subs - 1), subs)})
+        return carry
+
+    lax.fori_loop(1, subs, greet_sub, 0)
+    lax.fori_loop(1, groups, greet_grp, 0)
     for c in range(chunks):
         load_rs(c).start()
     for load in small:
@@ -105,21 +120,6 @@
     load_g.start()
     load_k.start()
     load_s.start()
-    barrier = pltpu.get_barrier_semaphore()
-
-    def greet(sem, where):
-        pl.semaphore_signal(sem, inc=1, device_id=where, device_id_type=MESH)
-
-    def greet_grp(d, carry):
-        greet(barrier, {"grp": lax.rem(g + d, groups)})
-        return carry
-
-    def greet_sub(d, carry):
-        greet(barrier, {"sub": lax.rem(j + d, subs)})
-        return carry
-
-    lax.fori_loop(1, subs, greet_sub, 0)
-    lax.fori_loop(1, groups, greet_grp, 0)
 
     def cast(c):
         load_rs(c).wait()
@@ -157,11 +157,6 @@
             sc["rcin"][j] = sc["rc"][b]
 
         return carry
-
-    pl.semaphore_wait(barrier, groups - 1 + subs - 1)
-    lax.fori_loop(0, blocks, rc_send, 0)
-    for c in range(AHEAD):
-        rb_copy(c).start()
 
     load_g.wait()
     sc["gt"][...] = sc["gm"][...].T
@@ -179,6 +174,11 @@
     sc["coef"][...] = jnp.broadcast_to(coef, (LANES, face)).T
     sc["ra"][...] = jnp.zeros_like(sc["ra"])
 
+    pl.semaphore_wait(barrier, groups - 1 + subs - 1)
+    lax.fori_loop(0, blocks, rc_send, 0)
+    for c in range(AHEAD):
+        rb_copy(c).start()
+
     pt_copy = remote(sc["pt"], sc["ptl"], sc["el_ss"].at[0], sc["el_rs"].at[0], {"sub": right})
     el_copy = remote(sc["el"], sc["ell"], sc["el_ss"].at[1], sc["el_rs"].at[1], {"sub": right})
     if head:
@@ -326,7 +326,7 @@
 
         def start(own):
             def go(d, carry):
-                copy(lax.rem(me + d, count)).start()
+                copy(lax.rem(me + 1 + lax.rem(d + count // 3, count - 1), count)).start()
                 return carry
 
             lax.fori_loop(1, count, go, 0)

time: 78.6 us -> 78.3 us (level)
  no operation moved by 1% of the time
where the time goes in v4:
time: 78.3 us; the launch traced here: 78.2 us
  Pallas kernels  77.5 us (99%)
    pallas_call x1, Pallas kernels, body(): pl.pallas_call(wrapped, out_shape=(held, held), in_specs=[hbm] * 7, out_s...  75.5 us
    pallas_call x1, Pallas kernels, body(): pl.pallas_call(write_out, out_shape=(out, out), in_specs=[vmem, vmem], ou...  2.03 us

profile of v4, /device:TPU:1, one launch (start us, length us, event | category | flops | bytes accessed | tf_op | source)
XLA Modules:
  0.0 78.2 jit_solution(7471588711546773835)
XLA Ops:
  0.6 75.5 %bddc_step.1 = (f32[256,2048]{1,0:T(8,128)S(1)}, f32[256,2048]{1,0:T(8,128)S(1)}) custom-call(f32[256,2048]{1,0:T(8,128)} %refs_0_.1, bf16[512,512]{1,0:T(8,128)(2,1)} %refs_1_.1, bf16[512,512]{1,0:T(8,128)(2,1)} %refs_2_.1, f32[256,256]{1,0:T(8,128)} %refs_3_.1, s32[1,8]{1,0:T(1,128)} %refs_4_.1, s32[1,256]{1,0:T(1,128)} %bitcast.2, f32[1,4]{1,0:T(1,128)} %bitcast.3), custom_call_target="tpu_custom_call" | custom-call | tf_op jit(solution)/shard_map/bddc_step/pallas_call | solution.py:566
  76.2 2.0 %write_out.1 = (f32[256,2048]{1,0:T(8,128)}, f32[256,2048]{1,0:T(8,128)}) custom-call(f32[256,2048]{1,0:T(8,128)S(1)} %get-tuple-element.4.sol_ref, f32[256,2048]{1,0:T(8,128)S(1)} %get-tuple-element.5.res_ref), custom_call_target="tpu_custom_call" | custom-call | tf_op jit(solution)/shard_map/write_out/pallas_call | solution.py:577

commit v5 on v4

--- a/solution.py
+++ b/solution.py
@@ -147,7 +147,9 @@
             sc["rc"].at[b], sc["rcin"].at[j], sc["rc_ss"].at[b], sc["rc_rs"], {"sub": b * stride}
         )
 
-    def rc_send(b, carry):
+    def rc_send(turn, carry):
+        b = lax.rem(turn + j // stride, blocks)
+
         @pl.when(b * stride != j)
         def _():
             rc_copy(b).start()
@@ -213,7 +215,7 @@
         @pl.when(is_solver)
         def _():
             def h_send(d, carry):
-                h_copy(lax.rem(j + d, subs)).start()
+                h_copy(lax.rem(j + 1 + lax.rem(d + subs // 3, subs - 1), subs)).start()
                 return carry
 
             lax.fori_loop(1, subs, h_send, 0)

time: 78.3 us -> 78.3 us (level)
  no operation moved by 1% of the time
where the time goes in v5:
time: 78.3 us; the launch traced here: 78.2 us
  Pallas kernels  77.5 us (99%)
    pallas_call x1, Pallas kernels, body(): pl.pallas_call(wrapped, out_shape=(held, held), in_specs=[hbm] * 7, out_s...  75.5 us
    pallas_call x1, Pallas kernels, body(): pl.pallas_call(write_out, out_shape=(out, out), in_specs=[vmem, vmem], ou...  2.03 us

profile of v5, /device:TPU:1, one launch (start us, length us, event | category | flops | bytes accessed | tf_op | source)
XLA Modules:
  0.0 78.2 jit_solution(9670884337967161358)
XLA Ops:
  0.6 75.5 %bddc_step.1 = (f32[256,2048]{1,0:T(8,128)S(1)}, f32[256,2048]{1,0:T(8,128)S(1)}) custom-call(f32[256,2048]{1,0:T(8,128)} %refs_0_.1, bf16[512,512]{1,0:T(8,128)(2,1)} %refs_1_.1, bf16[512,512]{1,0:T(8,128)(2,1)} %refs_2_.1, f32[256,256]{1,0:T(8,128)} %refs_3_.1, s32[1,8]{1,0:T(1,128)} %refs_4_.1, s32[1,256]{1,0:T(1,128)} %bitcast.2, f32[1,4]{1,0:T(1,128)} %bitcast.3), custom_call_target="tpu_custom_call" | custom-call | tf_op jit(solution)/shard_map/bddc_step/pallas_call | solution.py:568
  76.1 2.0 %write_out.1 = (f32[256,2048]{1,0:T(8,128)}, f32[256,2048]{1,0:T(8,128)}) custom-call(f32[256,2048]{1,0:T(8,128)S(1)} %get-tuple-element.4.sol_ref, f32[256,2048]{1,0:T(8,128)S(1)} %get-tuple-element.5.res_ref), custom_call_target="tpu_custom_call" | custom-call | tf_op jit(solution)/shard_map/write_out/pallas_call | solution.py:579
